TPU v7x, 32 devices: a whole 2x2x4 slice. The times are simulated.
32 devices in a mesh: band: 2 (over x), pw: 16 (over z, y, core).
Axes of the slice: x: 2, y: 2, z: 4, core: 2. Of those that a mesh axis runs over, the one named last changes fastest.
Arguments:
- basis_re: float32 [8, 2, 2, 4096], P(None, None, 'band', 'pw'), may hold values from -24 to 24
- basis_im: float32 [8, 2, 2, 4096], P(None, None, 'band', 'pw'), may hold values from -24 to 24
- potential: float32 [192, 192, 192], P('pw'), may hold values from -15 to 15
- kinetic: float32 [2, 4096], P(None, 'pw'), may hold values from 0 to 30
- form_factors: float32 [8, 2, 4096], P(None, None, 'pw'), may hold values from -12 to 12
- channel_strength: float32 [8], replicated, may hold values from -4 to 4
- sphere_map: int32 [2, 4096], P(None, 'pw'), may hold values from 0 to 1535, as said below
- column_map: int32 [128], replicated, may hold values from 0 to 36863, as said below
- atom_sites: int32 [3, 512], replicated, may hold values from 0 to 191
Outputs:
- next_re: float32 [2, 2, 4096], P(None, 'band', 'pw')
- next_im: float32 [2, 2, 4096], P(None, 'band', 'pw')
- coeffs_re: float32 [8, 2, 2], replicated
- coeffs_im: float32 [8, 2, 2], replicated
- chol_re: float32 [2, 2], replicated
- chol_im: float32 [2, 2], replicated
Inputs may be any that keep to these rules, and one draw needn't show every extreme that they name: `sphere_map`: within each group of 256 consecutive values of the second index, the entries over both indices are distinct. `column_map`: all entries are distinct.
All inputs are finite; a program needn't handle non-finite values.
Results may differ from a plain program's by a relative error of at most 0.0015.
The roundings to bfloat16 on the way count: a program that leaves them out, or rounds other values in their place, can miss the bound.
Values sent between devices are 32-bit elements; how exact they have to be, the bound alone decides.
A program may use at most 128 MiB of HBM per device.

v0:
```python
import functools
import math

import jax
import jax.numpy as jnp
import numpy as np
from jax import lax
from jax.experimental import pallas as pl
from jax.experimental.pallas import tpu as pltpu
from jax.sharding import PartitionSpec as P

f32 = jnp.float32
bf16 = jnp.bfloat16
NN = (((1,), (0,)), ((), ()))
NT = (((1,), (1,)), ((), ()))
TN = (((0,), (0,)), ((), ()))


def dot(left, right, dims):
    return lax.dot_general(left, right, dims, preferred_element_type=f32)


def exact_dot(left, right, dims):
    return lax.dot_general(
        left, right, dims, precision=lax.Precision.HIGHEST, preferred_element_type=f32
    )


def halves(value):
    high = value.astype(bf16)
    return high, (value - high.astype(f32)).astype(bf16)


def dot_split(value, table_high, table_low, dims):
    high, low = halves(value)
    return (
        dot(high, table_high, dims) + dot(low, table_high, dims) + dot(high, table_low, dims)
    )


def table_halves(table):
    table = np.asarray(table, np.float32)
    high = table.astype(jnp.bfloat16)
    low = (table - high.astype(np.float32)).astype(jnp.bfloat16)
    return jnp.asarray(high), jnp.asarray(low)


def host_tables(grid, planes, wave_groups, span):
    ticks = np.arange(grid)
    angle = (ticks[:, None] * ticks[None, :] % grid) * (2.0 * math.pi / grid)
    cos, sin = np.cos(angle), np.sin(angle)
    lanes = wave_groups * span
    spread = np.zeros((2, grid, wave_groups, 2, span // 2))
    split_cos = cos.reshape(grid, wave_groups, planes)
    split_sin = sin.reshape(grid, wave_groups, planes)
    spread[0, :, :, 0, :planes] = split_cos
    spread[0, :, :, 1, :planes] = split_sin
    spread[1, :, :, 0, :planes] = -split_sin
    spread[1, :, :, 1, :planes] = split_cos
    spread = spread.reshape(2, grid, lanes)
    back = np.zeros((2, wave_groups, 2, span // 2, grid))
    scale = 1.0 / float(grid) ** 3
    rows_cos = cos.reshape(wave_groups, planes, grid) * scale
    rows_sin = sin.reshape(wave_groups, planes, grid) * scale
    back[0, :, 0, :planes] = rows_cos
    back[0, :, 1, :planes] = rows_sin
    back[1, :, 0, :planes] = -rows_sin
    back[1, :, 1, :planes] = rows_cos
    back = back.reshape(2, lanes, grid)
    return (
        *table_halves(spread),
        *table_halves(back),
        *table_halves(np.stack([cos, sin])),
    )


def cos_sin_192(turns, grid):
    quarter = grid // 4
    step = jnp.floor(turns * (1.0 / quarter) + 0.5)
    rest = turns - step * quarter
    x = rest * (2.0 * math.pi / grid)
    x2 = x * x
    sine = x + x * x2 * (
        -1.6666654611e-1 + x2 * (8.3321608736e-3 + x2 * -1.9515295891e-4)
    )
    cosine = (
        1.0
        - 0.5 * x2
        + x2 * x2 * (4.166664568298827e-2 + x2 * (-1.388731625493765e-3 + x2 * 2.443315711809948e-5))
    )
    count = step.astype(jnp.int32)
    odd = (count & 1) == 1
    flip_cos = ((count + 1) & 2) == 2
    flip_sin = (count & 2) == 2
    out_cos = jnp.where(odd, sine, cosine)
    out_sin = jnp.where(odd, cosine, sine)
    return (
        jnp.where(flip_cos, -out_cos, out_cos),
        jnp.where(flip_sin, -out_sin, out_sin),
    )


def kernel(
    cfg,
    pot_ref,
    basis_re_ref,
    basis_im_ref,
    kin_ref,
    form_ref,
    strength_ref,
    sphere_ref,
    cmap_ref,
    sites_ref,
    t1h_ref,
    t1l_ref,
    f2h_ref,
    f2l_ref,
    dh_ref,
    dl_ref,
    next_re_ref,
    next_im_ref,
    coef_re_ref,
    coef_im_ref,
    chol_re_ref,
    chol_im_ref,
    y1_buf,
    col_buf,
    col_s,
    ps_send,
    ps_recv,
    sc_send,
    sc_buf,
    out_s,
    out_send,
    out_buf,
    co_send,
    co_buf,
    gr_send,
    gr_buf,
    ct_s,
    phase_cos,
    phase_sin,
    send_sem,
    recv_sem,
):
    n_band, n_pw, slab, blocks, channels, planes, grid, col_dev, span, group = cfg
    n_dev = n_band * n_pw
    vectors = blocks * slab
    columns = n_pw * col_dev
    per_tile = 128 // span
    tiles = n_pw * span // 128
    atoms = sites_ref.shape[1]
    rows = 2 * slab * channels
    half_rows = slab * channels
    waves = kin_ref.shape[1]
    total_waves = n_dev * waves
    root_waves = math.sqrt(total_waves)
    s = lax.axis_index("band")
    q = lax.axis_index("pw")
    me = s * n_pw + q

    def coords(device):
        return (device // n_pw, lax.rem(device, n_pw))

    barrier = pltpu.get_barrier_semaphore()

    def greet(k, carry):
        device = lax.rem(me + k, n_dev)
        pl.semaphore_signal(
            barrier, inc=1, device_id=coords(device), device_id_type=pl.DeviceIdType.MESH
        )
        return carry

    lax.fori_loop(1, n_dev, greet, 0)

    def push(source, target, sem, limit=n_dev):
        def one(k, carry):
            device = lax.rem(me + k, n_dev)

            def go():
                pltpu.make_async_remote_copy(
                    src_ref=source(device),
                    dst_ref=target,
                    send_sem=send_sem.at[sem],
                    recv_sem=recv_sem.at[sem],
                    device_id=coords(device),
                    device_id_type=pl.DeviceIdType.MESH,
                ).start()

            if limit < n_dev:
                pl.when(device < limit)(go)
            else:
                go()
            return carry

        lax.fori_loop(1, n_dev, one, 0)

    def take(buf, sem, count):
        view = buf.at[pl.ds(0, count)]
        pltpu.make_async_copy(view, view, sem).wait()

    cells = sphere_ref[pl.ds(s, 1), :].astype(f32)
    depth = jnp.floor((cells + 0.5) * (1.0 / col_dev))
    column = cells - depth * col_dev
    mask = (
        lax.broadcasted_iota(jnp.int32, (col_dev, waves), 0) == column.astype(jnp.int32)
    ).astype(f32)
    one_hot = jnp.where(
        lax.broadcasted_iota(jnp.int32, (grid, waves), 0) == depth.astype(jnp.int32), 1.0, 0.0
    ).astype(bf16)
    flat_re = basis_re_ref[...]
    flat_im = basis_im_ref[...]
    psi_re = flat_re[vectors - slab :]
    psi_im = flat_im[vectors - slab :]
    placed = jnp.concatenate(
        [mask * psi_re[b : b + 1] for b in range(slab)]
        + [mask * psi_im[b : b + 1] for b in range(slab)],
        0,
    )
    high, low = halves(placed)
    field = dot(high, one_hot, NT) + dot(low, one_hot, NT)
    half = slab * col_dev
    spread = dot_split(field[:half], t1h_ref[0], t1l_ref[0], NN) + dot_split(
        field[half:], t1h_ref[1], t1l_ref[1], NN
    )
    for b in range(slab):
        for t in range(tiles):
            y1_buf[b, t] = spread[b * col_dev : (b + 1) * col_dev, t * 128 : (t + 1) * 128]

    pl.semaphore_wait(barrier, n_dev - 1)
    push(
        lambda device: y1_buf.at[device // n_pw, lax.rem(device, n_pw) // per_tile],
        col_buf.at[me],
        0,
    )
    col_buf[me] = y1_buf[s, q // per_tile]

    col_x = cmap_ref[...].astype(f32)
    all_x = jnp.floor((col_x + 0.5) * (1.0 / grid))
    all_y = col_x - all_x * grid
    own = lax.broadcasted_iota(jnp.int32, (col_dev, columns), 1) == (
        q * col_dev + lax.broadcasted_iota(jnp.int32, (col_dev, columns), 0)
    )
    own_x = jnp.sum(jnp.where(own, all_x, 0.0), 1, keepdims=True)
    own_y = jnp.sum(jnp.where(own, all_y, 0.0), 1, keepdims=True)
    wave_x = jnp.sum(mask * own_x, 0, keepdims=True)
    wave_y = jnp.sum(mask * own_y, 0, keepdims=True)
    places = jnp.concatenate([depth, wave_x, wave_y, jnp.zeros((5, waves), f32)], 0)
    sites = jnp.concatenate([sites_ref[...].astype(f32), jnp.zeros((5, atoms), f32)], 0)
    turns = dot(places.T.astype(bf16), sites.astype(bf16), NN)
    cosine, sine = cos_sin_192(turns, grid)
    phase_cos[...] = cosine.astype(bf16)
    phase_sin[...] = sine.astype(bf16)
    form = form_ref[:, pl.ds(s, 1), :].reshape(channels, waves)
    weighted = jnp.concatenate(
        [form * psi_re[b : b + 1] for b in range(slab)]
        + [form * psi_im[b : b + 1] for b in range(slab)],
        0,
    ).astype(bf16)
    with_cos = dot(weighted, phase_cos[...], NN)
    with_sin = dot(weighted, phase_sin[...], NN)
    sums = jnp.concatenate(
        [
            with_cos[:half_rows] - with_sin[half_rows:],
            with_sin[:half_rows] + with_cos[half_rows:],
        ],
        0,
    )
    parts = atoms // 128
    for t in range(parts):
        ps_send[:, t, :] = sums[:, t * 128 : (t + 1) * 128]
    push(lambda device: ps_send.at[device], ps_recv.at[me], 1, rows)

    def at_columns(position):
        ticks = lax.broadcasted_iota(jnp.int32, (grid, columns), 0)
        chosen = jnp.where(ticks == position.astype(jnp.int32), 1.0, 0.0).astype(bf16)
        return [dot(table[i], chosen, NN) for table in (dh_ref, dl_ref) for i in (0, 1)]

    xch, xsh, xcl, xsl = at_columns(all_x)
    x_cos = xch + xcl
    x_sin = xsh + xsl
    ych, ysh, ycl, ysl = [part.astype(bf16) for part in at_columns(all_y)]
    mre_high = jnp.concatenate([ych, -ysh], 1)
    mre_low = jnp.concatenate([ycl, -ysl], 1)
    mim_high = jnp.concatenate([ysh, ych], 1)
    mim_low = jnp.concatenate([ysl, ycl], 1)

    out_s[...] = jnp.zeros_like(out_s)
    base = lax.rem(q, per_tile) * span

    take(col_buf, recv_sem.at[0], n_dev - 1)
    gathered = col_buf[0:n_pw]
    for b in range(1, n_band):
        gathered = gathered + col_buf[b * n_pw : (b + 1) * n_pw]
    col_s[...] = gathered.reshape(columns, 128).T

    def own_row():
        ps_recv[me] = ps_send[me]
        take(ps_recv, recv_sem.at[1], n_dev - 1)
        total = jnp.sum(ps_recv[...], 0)
        strength = strength_ref[lax.rem(me, channels)]
        sc_send[...] = strength * (total * (1.0 / root_waves)) * (1.0 / root_waves)
        sc_buf[me] = sc_send[...]
        push(lambda device: sc_send, sc_buf.at[me], 2)

    if rows < n_dev:
        pl.when(me < rows)(own_row)
    else:
        own_row()

    def some_planes(step, carry):
        first = step * group
        mixed = []
        for i in range(group):
            part_re = col_s[pl.ds(base + first + i, 1), :]
            part_im = col_s[pl.ds(base + span // 2 + first + i, 1), :]
            mixed.append(
                jnp.concatenate(
                    [x_cos * part_re - x_sin * part_im, x_cos * part_im + x_sin * part_re], 1
                )
            )
        mixed = jnp.concatenate(mixed, 0)
        field_re = dot_split(mixed, mre_high, mre_low, NT)
        field_im = dot_split(mixed, mim_high, mim_low, NT)
        weight = pot_ref[pl.ds(first, group)].reshape(group * grid, grid)
        back = dot_split(field_re * weight, mre_high, mre_low, NN) + dot_split(
            field_im * weight, mim_high, mim_low, NN
        )
        for i in range(group):
            back_re = back[i * grid : (i + 1) * grid, :columns]
            back_im = back[i * grid : (i + 1) * grid, columns:]
            out_s[pl.ds(base + first + i, 1), :] = jnp.sum(
                x_cos * back_re + x_sin * back_im, 0, keepdims=True
            )
            out_s[pl.ds(base + span // 2 + first + i, 1), :] = jnp.sum(
                x_cos * back_im - x_sin * back_re, 0, keepdims=True
            )
        return carry

    lax.fori_loop(0, planes // group, some_planes, 0)
    out_send[...] = out_s[...].T.reshape(n_pw, col_dev, 128)
    push(lambda device: out_send.at[lax.rem(device, n_pw)], out_buf.at[me], 3)
    out_buf[me] = out_send[q]

    if rows < n_dev:
        pl.when(me < rows)(lambda: take(sc_buf, recv_sem.at[2], rows - 1))
        pl.when(me >= rows)(lambda: take(sc_buf, recv_sem.at[2], rows))
    else:
        take(sc_buf, recv_sem.at[2], rows - 1)
    scaled = jnp.concatenate([sc_buf[:, t, :] for t in range(parts)], 1)
    scaled_re = scaled[:half_rows]
    scaled_im = scaled[half_rows:]
    near = dot(
        jnp.concatenate([scaled_re, scaled_im], 0).astype(bf16), phase_cos[...], NT
    ) + dot(jnp.concatenate([scaled_im, -scaled_re], 0).astype(bf16), phase_sin[...], NT)
    near = [
        jnp.sum(form * near[i * channels : (i + 1) * channels], 0, keepdims=True)
        for i in range(2 * slab)
    ]
    psi_all = jnp.concatenate([psi_re, psi_im], 0)
    image = kin_ref[pl.ds(s, 1), :] * psi_all + jnp.concatenate(near, 0)

    take(out_buf, recv_sem.at[3], n_dev - 1)
    lines = []
    for b in range(slab):
        line = []
        for t in range(tiles):
            begin = b * n_pw + t * per_tile
            line.append(jnp.sum(out_buf[begin : begin + per_tile], 0))
        lines.append(jnp.concatenate(line, 1))
    lines = jnp.concatenate(lines, 0)
    high, low = halves(lines)
    depths = [
        dot(high, f2h_ref[i], NN) + dot(low, f2h_ref[i], NN) + dot(high, f2l_ref[i], NN)
        for i in (0, 1)
    ]
    high, low = halves(jnp.concatenate(depths, 0))
    read = dot(high, one_hot, NN) + dot(low, one_hot, NN)
    local = [
        jnp.sum(mask * read[i * col_dev : (i + 1) * col_dev], 0, keepdims=True)
        for i in range(2 * slab)
    ]
    image = image + jnp.concatenate(local, 0)

    def doubled(wave):
        first, second = wave[:slab], wave[slab:]
        return jnp.concatenate(
            [
                jnp.concatenate([first, second], 1),
                jnp.concatenate([second, -first], 1),
            ],
            0,
        )

    span_rows = jnp.concatenate([flat_re, flat_im], 0)
    span_double = jnp.concatenate(
        [jnp.concatenate([flat_re, flat_im], 1), jnp.concatenate([flat_im, -flat_re], 1)], 0
    )
    part = exact_dot(doubled(image), span_double, NT) * (1.0 / total_waves)
    co_send[...] = jnp.zeros_like(co_send)
    co_send[:, 0 : 2 * vectors] = part
    push(lambda device: co_send, co_buf.at[me], 4)
    co_buf[me] = co_send[...]
    take(co_buf, recv_sem.at[4], n_dev - 1)
    coef = jnp.sum(co_buf[...], 0)
    residue = image - exact_dot(coef[:, : 2 * vectors], span_rows, NN)

    residue_double = doubled(residue)
    part = exact_dot(residue_double, residue_double, NT) * (1.0 / total_waves)
    gr_send[...] = jnp.zeros_like(gr_send)
    gr_send[:, 0 : 2 * slab] = part
    push(lambda device: gr_send, gr_buf.at[me], 5)
    gr_buf[me] = gr_send[...]

    pad = -coef.shape[0] % 8
    tall = jnp.concatenate([coef, jnp.zeros((pad, coef.shape[1]), f32)], 0) if pad else coef
    ct_s[...] = tall.T
    for k in range(slab):
        line = ct_s[pl.ds(k, blocks, stride=slab), :]
        coef_re_ref[:, k, :] = line[:, :slab]
        coef_im_ref[:, k, :] = line[:, slab : 2 * slab]

    take(gr_buf, recv_sem.at[5], n_dev - 1)
    gram = jnp.sum(gr_buf[...], 0)

    lane = lax.broadcasted_iota(jnp.int32, (1, gram.shape[1]), 1)

    def entry(row, index):
        return jnp.sum(jnp.where(lane == index, row, 0.0), 1, keepdims=True)

    def moved(row):
        return pltpu.roll(row, gram.shape[1] - slab, 1)

    upper = []
    for r in range(slab):
        total_re = gram[r : r + 1]
        total_im = moved(gram[r : r + 1])
        for up_re, up_im in upper:
            a_re, a_im = entry(up_re, r), entry(up_im, r)
            total_re, total_im = (
                total_re - (a_re * up_re + a_im * up_im),
                total_im - (a_re * up_im - a_im * up_re),
            )
        pivot = jnp.sqrt(entry(total_re, r))
        ok = lane < slab
        upper.append(
            (
                jnp.where((lane >= r) & ok, total_re / pivot, 0.0),
                jnp.where((lane > r) & ok, total_im / pivot, 0.0),
            )
        )
    chol_re_ref[...] = jnp.concatenate([u[0] for u in upper], 0)[:, :slab]
    chol_im_ref[...] = jnp.concatenate([u[1] for u in upper], 0)[:, :slab]
    solved = []
    for e in range(slab):
        row_re = residue[e : e + 1]
        row_im = residue[slab + e : slab + e + 1]
        for b in range(e):
            r_re, r_im = entry(upper[b][0], e), entry(upper[b][1], e)
            row_re, row_im = (
                row_re - (solved[b][0] * r_re - solved[b][1] * r_im),
                row_im - (solved[b][0] * r_im + solved[b][1] * r_re),
            )
        inverse = 1.0 / entry(upper[e][0], e)
        solved.append((row_re * inverse, row_im * inverse))
    next_re_ref[...] = jnp.concatenate([x[0] for x in solved], 0)
    next_im_ref[...] = jnp.concatenate([x[1] for x in solved], 0)

    take(col_buf, send_sem.at[0], n_dev - 1)
    if rows < n_dev:
        pl.when(me < rows)(lambda: take(ps_recv, send_sem.at[1], rows - 1))
        pl.when(me >= rows)(lambda: take(ps_recv, send_sem.at[1], rows))
        pl.when(me < rows)(lambda: take(ps_recv, send_sem.at[2], n_dev - 1))
    else:
        take(ps_recv, send_sem.at[1], rows - 1)
        take(ps_recv, send_sem.at[2], n_dev - 1)
    take(out_buf, send_sem.at[3], n_dev - 1)
    take(co_buf, send_sem.at[4], n_dev - 1)
    take(gr_buf, send_sem.at[5], n_dev - 1)


def body(
    basis_re,
    basis_im,
    potential,
    kinetic,
    form_factors,
    channel_strength,
    sphere_map,
    column_map,
    atom_sites,
):
    blocks, slab, _, waves = basis_re.shape
    n_band = lax.axis_size("band")
    n_pw = lax.axis_size("pw")
    n_dev = n_band * n_pw
    planes, grid, _ = potential.shape
    channels = form_factors.shape[0]
    columns = column_map.shape[0]
    col_dev = columns // n_pw
    atoms = atom_sites.shape[1]
    vectors = blocks * slab
    rows = 2 * slab * channels
    span = 8
    while span < 2 * planes:
        span *= 2
    group = max(g for g in (1, 2, 3, 4) if planes % g == 0)
    tiles = n_pw * span // 128
    wide = -(-2 * vectors // 128) * 128
    assert slab == n_band and rows <= n_dev and n_pw * span % 128 == 0
    tables = host_tables(grid, planes, n_pw, span)
    cfg = (n_band, n_pw, slab, blocks, channels, planes, grid, col_dev, span, group)
    vmem = pl.BlockSpec(memory_space=pltpu.VMEM)
    smem = pl.BlockSpec(memory_space=pltpu.SMEM)
    parts = atoms // 128
    outs = pl.pallas_call(
        functools.partial(kernel, cfg),
        out_shape=[
            jax.ShapeDtypeStruct((slab, waves), f32),
            jax.ShapeDtypeStruct((slab, waves), f32),
            jax.ShapeDtypeStruct((blocks, slab, slab), f32),
            jax.ShapeDtypeStruct((blocks, slab, slab), f32),
            jax.ShapeDtypeStruct((slab, slab), f32),
            jax.ShapeDtypeStruct((slab, slab), f32),
        ],
        in_specs=[vmem] * 5 + [smem] + [vmem] * 9,
        out_specs=[vmem] * 6,
        scratch_shapes=[
            pltpu.VMEM((slab, tiles, col_dev, 128), f32),
            pltpu.VMEM((n_dev, col_dev, 128), f32),
            pltpu.VMEM((128, columns), f32),
            pltpu.VMEM((rows, parts, 128), f32),
            pltpu.VMEM((n_dev, parts, 128), f32),
            pltpu.VMEM((parts, 128), f32),
            pltpu.VMEM((rows, parts, 128), f32),
            pltpu.VMEM((128, columns), f32),
            pltpu.VMEM((n_pw, col_dev, 128), f32),
            pltpu.VMEM((n_dev, col_dev, 128), f32),
            pltpu.VMEM((2 * slab, wide), f32),
            pltpu.VMEM((n_dev, 2 * slab, wide), f32),
            pltpu.VMEM((2 * slab, 128), f32),
            pltpu.VMEM((n_dev, 2 * slab, 128), f32),
            pltpu.VMEM((wide, -(-2 * slab // 8) * 8), f32),
            pltpu.VMEM((waves, atoms), bf16),
            pltpu.VMEM((waves, atoms), bf16),
            pltpu.SemaphoreType.DMA((6,)),
            pltpu.SemaphoreType.DMA((6,)),
        ],
        compiler_params=pltpu.CompilerParams(
            collective_id=0, has_side_effects=True, vmem_limit_bytes=56 * 2**20
        ),
    )(
        potential,
        basis_re.reshape(vectors, waves),
        basis_im.reshape(vectors, waves),
        kinetic,
        form_factors,
        channel_strength,
        sphere_map,
        column_map.reshape(1, columns),
        atom_sites,
        *tables,
    )
    next_re, next_im, coef_re, coef_im, chol_re, chol_im = outs
    return (
        next_re.reshape(slab, 1, waves),
        next_im.reshape(slab, 1, waves),
        coef_re,
        coef_im,
        chol_re,
        chol_im,
    )


def solution(mesh):
    return jax.shard_map(
        body,
        mesh=mesh,
        in_specs=(
            P(None, None, "band", "pw"),
            P(None, None, "band", "pw"),
            P("pw", None, None),
            P(None, "pw"),
            P(None, None, "pw"),
            P(),
            P(None, "pw"),
            P(),
            P(),
        ),
        out_specs=(P(None, "band", "pw"), P(None, "band", "pw"), P(), P(), P(), P()),
        check_vma=False,
    )
```

profile of v0, /device:TPU:0, one launch (start us, length us, event | category | flops | bytes accessed | tf_op | source)
XLA Modules:
  0.0 50.5 jit_solution(88756543951931213)
XLA Ops:
  0.6 0.8 %reduce = f32[8,2,256]{2,1,0:T(2,128)S(1)} reduce(f32[8,2,1,256]{3,2,1,0:T(1,128)} %param.15, f32[]{:T(128)} %constant.21), dimensions={2}, to_apply=%param.15.reduce_sub_computation | reduce | bytes 32772 | tf_op args[0]
  1.4 0.6 %reshape.27.basis_re_ref = f32[16,256]{1,0:T(8,128)} reshape(f32[8,2,256]{2,1,0:T(2,128)S(1)} %reduce) | data formatting | bytes 32768 | tf_op jit(solution)/shard_map/reshape | solution.py:554
  2.0 0.8 %reduce.1 = f32[8,2,256]{2,1,0:T(2,128)S(1)} reduce(f32[8,2,1,256]{3,2,1,0:T(1,128)} %param.16, f32[]{:T(128)} %constant.21), dimensions={2}, to_apply=%param.16.reduce_sub_computation | reduce | bytes 32772 | tf_op args[1]
  2.8 0.6 %reshape.28.basis_im_ref = f32[16,256]{1,0:T(8,128)} reshape(f32[8,2,256]{2,1,0:T(2,128)S(1)} %reduce.1) | data formatting | bytes 32768 | tf_op jit(solution)/shard_map/reshape | solution.py:555
  3.4 39.4 %shard_map.190 = (f32[2,256]{1,0:T(2,128)}, f32[2,256]{1,0:T(2,128)}, f32[8,2,2]{2,1,0:T(2,128)}, f32[8,2,2]{2,1,0:T(2,128)}, f32[2,2]{1,0:T(2,128)}, /*index=5*/f32[2,2]{1,0:T(2,128)}) custom-call(f32[12,192,192]{2,1,0:T(8,128)} %pot_ref.1, f32[16,256]{1,0:T(8,128)} %reshape.27.basis_re_ref, f32[16,256]{1,0:T(8,128)} %reshape.28.basis_im_ref, ...), custom_call_target="tpu_custom_call" | custom-call | tf_op jit(solution)/shard_map/pallas_call | solution.py:516
  42.8 1.2 %copy.21 = f32[2,1,256]{2,1,0:T(1,128)} copy(f32[2,1,256]{2,0,1:T(2,128)} %bitcast.4) | data formatting | bytes 4096
  44.1 1.2 %copy.22 = f32[2,1,256]{2,1,0:T(1,128)} copy(f32[2,1,256]{2,0,1:T(2,128)} %bitcast.3) | data formatting | bytes 4096
  45.3 1.4 %copy.23 = f32[8,2,2]{0,2,1:T(2,128)} copy(f32[8,2,2]{2,1,0:T(2,128)} %get-tuple-element.20) | data formatting | bytes 256
  46.7 1.4 %copy.24 = f32[8,2,2]{0,2,1:T(2,128)} copy(f32[8,2,2]{2,1,0:T(2,128)} %get-tuple-element.21) | data formatting | bytes 256
  48.0 1.2 %copy.29 = f32[2,2]{1,0:T(2,128)} copy(f32[2,2]{1,0:T(2,128)} %get-tuple-element.34) | data formatting | bytes 32
  49.3 1.2 %copy.30 = f32[2,2]{1,0:T(2,128)} copy(f32[2,2]{1,0:T(2,128)} %get-tuple-element.35) | data formatting | bytes 32
where the time goes:
time: 51 us; the launch traced here: 50.5 us
  Pallas kernels  39.4 us (77%)
  local copies, waits for them, and re-layouts  8.88 us (17%)
  other arithmetic  1.53 us (3%)
  between operations  0.65 us (1%)
    pallas_call x1, Pallas kernels, body(): pl.pallas_call(functools.partial(kernel, cfg), out_shape=[jax.ShapeDtypeS...  39.4 us
    unnamed x6, local copies, waits for them, and re-layouts  7.66 us
    unnamed x2, other arithmetic  1.53 us

commit v1 on v0

--- a/solution.py
+++ b/solution.py
@@ -117,12 +117,7 @@
     f2l_ref,
     dh_ref,
     dl_ref,
-    next_re_ref,
-    next_im_ref,
-    coef_re_ref,
-    coef_im_ref,
-    chol_re_ref,
-    chol_im_ref,
+    packed_ref,
     y1_buf,
     col_buf,
     col_s,
@@ -137,11 +132,16 @@
     co_buf,
     gr_send,
     gr_buf,
-    ct_s,
     phase_cos,
     phase_sin,
+    pot_buf,
+    f2h_buf,
+    f2l_buf,
+    dh_buf,
+    dl_buf,
     send_sem,
     recv_sem,
+    load_sem,
 ):
     n_band, n_pw, slab, blocks, channels, planes, grid, col_dev, span, group = cfg
     n_dev = n_band * n_pw
@@ -159,41 +159,60 @@
     q = lax.axis_index("pw")
     me = s * n_pw + q
 
-    def coords(device):
-        return (device // n_pw, lax.rem(device, n_pw))
+    def wrap(value, size):
+        return jnp.where(value >= size, value - size, value)
+
+    def others(act):
+        for turn in range(n_band):
+            band = wrap(s + turn, n_band)
+
+            def one(k, carry):
+                act(band, wrap(q + k, n_pw))
+                return carry
+
+            lax.fori_loop(1, n_pw, one, 0, unroll=n_dev <= 64)
+            if turn:
+                act(band, q)
 
     barrier = pltpu.get_barrier_semaphore()
-
-    def greet(k, carry):
-        device = lax.rem(me + k, n_dev)
-        pl.semaphore_signal(
-            barrier, inc=1, device_id=coords(device), device_id_type=pl.DeviceIdType.MESH
+    others(
+        lambda band, pw: pl.semaphore_signal(
+            barrier, inc=1, device_id=(band, pw), device_id_type=pl.DeviceIdType.MESH
         )
-        return carry
-
-    lax.fori_loop(1, n_dev, greet, 0)
+    )
+    loads = [
+        pltpu.make_async_copy(source, target, load_sem.at[i])
+        for i, (source, target) in enumerate(
+            [
+                (dh_ref, dh_buf),
+                (dl_ref, dl_buf),
+                (pot_ref, pot_buf),
+                (f2h_ref, f2h_buf),
+                (f2l_ref, f2l_buf),
+            ]
+        )
+    ]
+    for load in loads:
+        load.start()
 
     def push(source, target, sem, limit=n_dev):
-        def one(k, carry):
-            device = lax.rem(me + k, n_dev)
-
+        def one(band, pw):
             def go():
                 pltpu.make_async_remote_copy(
-                    src_ref=source(device),
+                    src_ref=source(band, pw),
                     dst_ref=target,
                     send_sem=send_sem.at[sem],
                     recv_sem=recv_sem.at[sem],
-                    device_id=coords(device),
+                    device_id=(band, pw),
                     device_id_type=pl.DeviceIdType.MESH,
                 ).start()
 
             if limit < n_dev:
-                pl.when(device < limit)(go)
+                pl.when(band * n_pw + pw < limit)(go)
             else:
                 go()
-            return carry
-
-        lax.fori_loop(1, n_dev, one, 0)
+
+        others(one)
 
     def take(buf, sem, count):
         view = buf.at[pl.ds(0, count)]
@@ -208,8 +227,10 @@
     one_hot = jnp.where(
         lax.broadcasted_iota(jnp.int32, (grid, waves), 0) == depth.astype(jnp.int32), 1.0, 0.0
     ).astype(bf16)
-    flat_re = basis_re_ref[...]
-    flat_im = basis_im_ref[...]
+    flat_re, flat_im = [
+        jnp.concatenate([ref[j, k] for j in range(blocks) for k in range(slab)], 0)
+        for ref in (basis_re_ref, basis_im_ref)
+    ]
     psi_re = flat_re[vectors - slab :]
     psi_im = flat_im[vectors - slab :]
     placed = jnp.concatenate(
@@ -229,7 +250,7 @@
 
     pl.semaphore_wait(barrier, n_dev - 1)
     push(
-        lambda device: y1_buf.at[device // n_pw, lax.rem(device, n_pw) // per_tile],
+        lambda band, pw: y1_buf.at[band, pw // per_tile],
         col_buf.at[me],
         0,
     )
@@ -269,12 +290,15 @@
     parts = atoms // 128
     for t in range(parts):
         ps_send[:, t, :] = sums[:, t * 128 : (t + 1) * 128]
-    push(lambda device: ps_send.at[device], ps_recv.at[me], 1, rows)
+    push(lambda band, pw: ps_send.at[band * n_pw + pw], ps_recv.at[me], 1, rows)
+
+    loads[0].wait()
+    loads[1].wait()
 
     def at_columns(position):
         ticks = lax.broadcasted_iota(jnp.int32, (grid, columns), 0)
         chosen = jnp.where(ticks == position.astype(jnp.int32), 1.0, 0.0).astype(bf16)
-        return [dot(table[i], chosen, NN) for table in (dh_ref, dl_ref) for i in (0, 1)]
+        return [dot(table[i], chosen, NN) for table in (dh_buf, dl_buf) for i in (0, 1)]
 
     xch, xsh, xcl, xsl = at_columns(all_x)
     x_cos = xch + xcl
@@ -301,12 +325,14 @@
         strength = strength_ref[lax.rem(me, channels)]
         sc_send[...] = strength * (total * (1.0 / root_waves)) * (1.0 / root_waves)
         sc_buf[me] = sc_send[...]
-        push(lambda device: sc_send, sc_buf.at[me], 2)
+        push(lambda band, pw: sc_send, sc_buf.at[me], 2)
 
     if rows < n_dev:
         pl.when(me < rows)(own_row)
     else:
         own_row()
+
+    loads[2].wait()
 
     def some_planes(step, carry):
         first = step * group
@@ -322,7 +348,7 @@
         mixed = jnp.concatenate(mixed, 0)
         field_re = dot_split(mixed, mre_high, mre_low, NT)
         field_im = dot_split(mixed, mim_high, mim_low, NT)
-        weight = pot_ref[pl.ds(first, group)].reshape(group * grid, grid)
+        weight = pot_buf[pl.ds(first, group)].reshape(group * grid, grid)
         back = dot_split(field_re * weight, mre_high, mre_low, NN) + dot_split(
             field_im * weight, mim_high, mim_low, NN
         )
@@ -339,7 +365,7 @@
 
     lax.fori_loop(0, planes // group, some_planes, 0)
     out_send[...] = out_s[...].T.reshape(n_pw, col_dev, 128)
-    push(lambda device: out_send.at[lax.rem(device, n_pw)], out_buf.at[me], 3)
+    push(lambda band, pw: out_send.at[pw], out_buf.at[me], 3)
     out_buf[me] = out_send[q]
 
     if rows < n_dev:
@@ -360,6 +386,8 @@
     psi_all = jnp.concatenate([psi_re, psi_im], 0)
     image = kin_ref[pl.ds(s, 1), :] * psi_all + jnp.concatenate(near, 0)
 
+    loads[3].wait()
+    loads[4].wait()
     take(out_buf, recv_sem.at[3], n_dev - 1)
     lines = []
     for b in range(slab):
@@ -371,7 +399,7 @@
     lines = jnp.concatenate(lines, 0)
     high, low = halves(lines)
     depths = [
-        dot(high, f2h_ref[i], NN) + dot(low, f2h_ref[i], NN) + dot(high, f2l_ref[i], NN)
+        dot(high, f2h_buf[i], NN) + dot(low, f2h_buf[i], NN) + dot(high, f2l_buf[i], NN)
         for i in (0, 1)
     ]
     high, low = halves(jnp.concatenate(depths, 0))
@@ -399,7 +427,7 @@
     part = exact_dot(doubled(image), span_double, NT) * (1.0 / total_waves)
     co_send[...] = jnp.zeros_like(co_send)
     co_send[:, 0 : 2 * vectors] = part
-    push(lambda device: co_send, co_buf.at[me], 4)
+    push(lambda band, pw: co_send, co_buf.at[me], 4)
     co_buf[me] = co_send[...]
     take(co_buf, recv_sem.at[4], n_dev - 1)
     coef = jnp.sum(co_buf[...], 0)
@@ -409,19 +437,55 @@
     part = exact_dot(residue_double, residue_double, NT) * (1.0 / total_waves)
     gr_send[...] = jnp.zeros_like(gr_send)
     gr_send[:, 0 : 2 * slab] = part
-    push(lambda device: gr_send, gr_buf.at[me], 5)
+    push(lambda band, pw: gr_send, gr_buf.at[me], 5)
     gr_buf[me] = gr_send[...]
 
-    pad = -coef.shape[0] % 8
-    tall = jnp.concatenate([coef, jnp.zeros((pad, coef.shape[1]), f32)], 0) if pad else coef
-    ct_s[...] = tall.T
-    for k in range(slab):
-        line = ct_s[pl.ds(k, blocks, stride=slab), :]
-        coef_re_ref[:, k, :] = line[:, :slab]
-        coef_im_ref[:, k, :] = line[:, slab : 2 * slab]
+    count = 2 * slab
+    packed_ref[0:count] = residue
+    packed_ref[count : 2 * count, 0 : coef.shape[1]] = coef
 
     take(gr_buf, recv_sem.at[5], n_dev - 1)
-    gram = jnp.sum(gr_buf[...], 0)
+    packed_ref[2 * count : 3 * count, 0:128] = jnp.sum(gr_buf[...], 0)
+
+    take(col_buf, send_sem.at[0], n_dev - 1)
+    if rows < n_dev:
+        pl.when(me < rows)(lambda: take(ps_recv, send_sem.at[1], rows - 1))
+        pl.when(me >= rows)(lambda: take(ps_recv, send_sem.at[1], rows))
+        pl.when(me < rows)(lambda: take(ps_recv, send_sem.at[2], n_dev - 1))
+    else:
+        take(ps_recv, send_sem.at[1], rows - 1)
+        take(ps_recv, send_sem.at[2], n_dev - 1)
+    take(out_buf, send_sem.at[3], n_dev - 1)
+    take(co_buf, send_sem.at[4], n_dev - 1)
+    take(gr_buf, send_sem.at[5], n_dev - 1)
+
+
+def finish(
+    slab,
+    blocks,
+    packed_ref,
+    next_re_ref,
+    next_im_ref,
+    coef_re_ref,
+    coef_im_ref,
+    chol_re_ref,
+    chol_im_ref,
+):
+    count = 2 * slab
+    vectors = blocks * slab
+    residue = packed_ref[0:count]
+    gram = packed_ref[2 * count : 3 * count, 0:128]
+    pick = (
+        lax.broadcasted_iota(jnp.int32, (slab * blocks, vectors), 0),
+        lax.broadcasted_iota(jnp.int32, (slab * blocks, vectors), 1),
+    )
+    order = (pick[1] == lax.rem(pick[0], blocks) * slab + pick[0] // blocks).astype(f32)
+    for part, ref in ((0, coef_re_ref), (slab, coef_im_ref)):
+        line = exact_dot(
+            packed_ref[count + part : count + part + slab, 0:vectors], order, NT
+        )
+        for k in range(slab):
+            ref[k] = line[:, k * blocks : (k + 1) * blocks]
 
     lane = lax.broadcasted_iota(jnp.int32, (1, gram.shape[1]), 1)
 
@@ -463,20 +527,9 @@
             )
         inverse = 1.0 / entry(upper[e][0], e)
         solved.append((row_re * inverse, row_im * inverse))
-    next_re_ref[...] = jnp.concatenate([x[0] for x in solved], 0)
-    next_im_ref[...] = jnp.concatenate([x[1] for x in solved], 0)
-
-    take(col_buf, send_sem.at[0], n_dev - 1)
-    if rows < n_dev:
-        pl.when(me < rows)(lambda: take(ps_recv, send_sem.at[1], rows - 1))
-        pl.when(me >= rows)(lambda: take(ps_recv, send_sem.at[1], rows))
-        pl.when(me < rows)(lambda: take(ps_recv, send_sem.at[2], n_dev - 1))
-    else:
-        take(ps_recv, send_sem.at[1], rows - 1)
-        take(ps_recv, send_sem.at[2], n_dev - 1)
-    take(out_buf, send_sem.at[3], n_dev - 1)
-    take(co_buf, send_sem.at[4], n_dev - 1)
-    take(gr_buf, send_sem.at[5], n_dev - 1)
+    for e in range(slab):
+        next_re_ref[e] = solved[e][0]
+        next_im_ref[e] = solved[e][1]
 
 
 def body(
@@ -513,18 +566,13 @@
     vmem = pl.BlockSpec(memory_space=pltpu.VMEM)
     smem = pl.BlockSpec(memory_space=pltpu.SMEM)
     parts = atoms // 128
-    outs = pl.pallas_call(
+    anywhere = pl.BlockSpec(memory_space=pl.ANY)
+    lanes = n_pw * span
+    packed = pl.pallas_call(
         functools.partial(kernel, cfg),
-        out_shape=[
-            jax.ShapeDtypeStruct((slab, waves), f32),
-            jax.ShapeDtypeStruct((slab, waves), f32),
-            jax.ShapeDtypeStruct((blocks, slab, slab), f32),
-            jax.ShapeDtypeStruct((blocks, slab, slab), f32),
-            jax.ShapeDtypeStruct((slab, slab), f32),
-            jax.ShapeDtypeStruct((slab, slab), f32),
-        ],
-        in_specs=[vmem] * 5 + [smem] + [vmem] * 9,
-        out_specs=[vmem] * 6,
+        out_shape=jax.ShapeDtypeStruct((6 * slab, max(waves, wide)), f32),
+        in_specs=[anywhere] + [vmem] * 4 + [smem] + [vmem] * 5 + [anywhere] * 4,
+        out_specs=vmem,
         scratch_shapes=[
             pltpu.VMEM((slab, tiles, col_dev, 128), f32),
             pltpu.VMEM((n_dev, col_dev, 128), f32),
@@ -540,19 +588,24 @@
             pltpu.VMEM((n_dev, 2 * slab, wide), f32),
             pltpu.VMEM((2 * slab, 128), f32),
             pltpu.VMEM((n_dev, 2 * slab, 128), f32),
-            pltpu.VMEM((wide, -(-2 * slab // 8) * 8), f32),
             pltpu.VMEM((waves, atoms), bf16),
             pltpu.VMEM((waves, atoms), bf16),
+            pltpu.VMEM((planes, grid, grid), f32),
+            pltpu.VMEM((2, lanes, grid), bf16),
+            pltpu.VMEM((2, lanes, grid), bf16),
+            pltpu.VMEM((2, grid, grid), bf16),
+            pltpu.VMEM((2, grid, grid), bf16),
             pltpu.SemaphoreType.DMA((6,)),
             pltpu.SemaphoreType.DMA((6,)),
+            pltpu.SemaphoreType.DMA((5,)),
         ],
         compiler_params=pltpu.CompilerParams(
             collective_id=0, has_side_effects=True, vmem_limit_bytes=56 * 2**20
         ),
     )(
         potential,
-        basis_re.reshape(vectors, waves),
-        basis_im.reshape(vectors, waves),
+        basis_re,
+        basis_im,
         kinetic,
         form_factors,
         channel_strength,
@@ -561,12 +614,24 @@
         atom_sites,
         *tables,
     )
-    next_re, next_im, coef_re, coef_im, chol_re, chol_im = outs
+    next_re, next_im, coef_re, coef_im, chol_re, chol_im = pl.pallas_call(
+        functools.partial(finish, slab, blocks),
+        out_shape=[
+            jax.ShapeDtypeStruct((slab, 1, waves), f32),
+            jax.ShapeDtypeStruct((slab, 1, waves), f32),
+            jax.ShapeDtypeStruct((slab, slab, blocks), f32),
+            jax.ShapeDtypeStruct((slab, slab, blocks), f32),
+            jax.ShapeDtypeStruct((slab, slab), f32),
+            jax.ShapeDtypeStruct((slab, slab), f32),
+        ],
+        in_specs=[vmem],
+        out_specs=[vmem] * 6,
+    )(packed)
     return (
-        next_re.reshape(slab, 1, waves),
-        next_im.reshape(slab, 1, waves),
-        coef_re,
-        coef_im,
+        next_re,
+        next_im,
+        coef_re.transpose(2, 0, 1),
+        coef_im.transpose(2, 0, 1),
         chol_re,
         chol_im,
     )

time: 51 us -> 41.1 us (0.81)
  local copies, waits for them, and re-layouts: 8.88 us -> 0 us
  other arithmetic: 1.53 us -> 0 us
  Pallas kernels: 39.4 us -> 40.2 us
    unnamed x6 -> x0, local copies, waits for them, and re-layouts: 7.66 us -> none
    unnamed x2 -> x0, other arithmetic: 1.53 us -> none
    reshape x2 -> x0, local copies, waits for them, and re-layouts: 1.22 us -> none  [the longest x1 0.61 us: body(): basis_im.reshape(vectors, waves)]
    pallas_call x1 -> x2, Pallas kernels: 39.4 us -> 40.2 us  [the longest x1 38.5 us: body(): pl.pallas_call(functools.partial(kernel, cfg), out_shape=jax.ShapeDtypeSt...]
where the time goes in v1:
time: 41.1 us; the launch traced here: 40.8 us
  Pallas kernels  40.2 us (98%)
  between operations  0.64 us (2%)
    pallas_call x1, Pallas kernels, body(): pl.pallas_call(functools.partial(kernel, cfg), out_shape=jax.ShapeDtypeSt...  38.5 us
    pallas_call x1, Pallas kernels, body(): pl.pallas_call(functools.partial(finish, slab, blocks), out_shape=[jax.Sh...  1.66 us

profile of v1, /device:TPU:0, one launch (start us, length us, event | category | flops | bytes accessed | tf_op | source)
XLA Modules:
  0.0 40.8 jit_solution(9541675709085994454)
XLA Ops:
  0.6 38.5 %shard_map.190.packed_ref = f32[12,256]{1,0:T(8,128)} custom-call(f32[12,192,192]{2,1,0:T(8,128)} %pot_ref.1, f32[8,2,1,256]{3,2,1,0:T(1,128)} %basis_re_ref.1, f32[8,2,1,256]{3,2,1,0:T(1,128)} %basis_im_ref.1, f32[2,256]{1,0:T(2,128)} %kin_ref.1, f32[8,2,256]{2,1,0:T(2,128)} %form_ref.1, f32[8]{0:T(128)} %strength_ref.1, s32[2,256]{1,0:T(2,128)} %sphere_ref.1, ...), custom_call_target="tpu_custom_call" | custom-call | tf_op jit(solution)/shard_map/pallas_call | solution.py:571
  39.2 1.7 %shard_map.191 = (f32[2,1,256]{2,1,0:T(1,128)}, f32[2,1,256]{2,1,0:T(1,128)}, f32[2,2,8]{2,1,0:T(2,128)}, f32[2,2,8]{2,1,0:T(2,128)}, f32[2,2]{1,0:T(2,128)}, /*index=5*/f32[2,2]{1,0:T(2,128)}) custom-call(f32[12,256]{1,0:T(8,128)} %shard_map.190.packed_ref), custom_call_target="tpu_custom_call" | custom-call | tf_op jit(solution)/shard_map/pallas_call | solution.py:617

commit v2 on v1

--- a/solution.py
+++ b/solution.py
@@ -128,6 +128,7 @@
     out_s,
     out_send,
     out_buf,
+    row_pad,
     co_send,
     co_buf,
     gr_send,
@@ -149,6 +150,8 @@
     columns = n_pw * col_dev
     per_tile = 128 // span
     tiles = n_pw * span // 128
+    fold_rows = col_dev // per_tile
+    piece = fold_rows * n_pw
     atoms = sites_ref.shape[1]
     rows = 2 * slab * channels
     half_rows = slab * channels
@@ -244,23 +247,49 @@
     spread = dot_split(field[:half], t1h_ref[0], t1l_ref[0], NN) + dot_split(
         field[half:], t1h_ref[1], t1l_ref[1], NN
     )
+    block = lax.broadcasted_iota(jnp.int32, (col_dev, 128), 1) // span
+    diagonal = lax.broadcasted_iota(jnp.int32, (col_dev, 128), 0) // fold_rows == block
+
+    def turned(tile, turn):
+        shift = turn % per_tile * span
+        return pltpu.roll(tile, shift, 1) if shift else tile
+
     for b in range(slab):
         for t in range(tiles):
-            y1_buf[b, t] = spread[b * col_dev : (b + 1) * col_dev, t * 128 : (t + 1) * 128]
+            tile = spread[b * col_dev : (b + 1) * col_dev, t * 128 : (t + 1) * 128]
+            turns = [turned(tile, d) for d in range(per_tile)]
+            for j in range(per_tile):
+                message = turns[-j % per_tile]
+                for g in range(1, per_tile):
+                    message = jnp.where(block == g, turns[(g - j) % per_tile], message)
+                message = jnp.where(diagonal, message, 0.0)
+                shift = col_dev // 2
+                while shift >= fold_rows:
+                    message = message + pltpu.roll(message, shift, 0)
+                    shift //= 2
+                y1_buf[b, t * per_tile + j] = message[:fold_rows]
 
     pl.semaphore_wait(barrier, n_dev - 1)
     push(
-        lambda band, pw: y1_buf.at[band, pw // per_tile],
+        lambda band, pw: y1_buf.at[band, pw],
         col_buf.at[me],
         0,
     )
-    col_buf[me] = y1_buf[s, q // per_tile]
+    col_buf[me] = y1_buf[s, q]
 
     col_x = cmap_ref[...].astype(f32)
     all_x = jnp.floor((col_x + 0.5) * (1.0 / grid))
     all_y = col_x - all_x * grid
+    if columns <= 512:
+        spot = lax.broadcasted_iota(jnp.int32, (columns, columns), 1)
+        moved = lax.broadcasted_iota(jnp.int32, (columns, columns), 0) == (
+            lax.rem(spot, n_pw) * col_dev + spot // n_pw
+        )
+        both = jnp.concatenate([all_x, all_y, jnp.zeros((6, columns), f32)], 0)
+        both = dot(both.astype(bf16), jnp.where(moved, 1.0, 0.0).astype(bf16), NN)
+        all_x, all_y = both[0:1], both[1:2]
     own = lax.broadcasted_iota(jnp.int32, (col_dev, columns), 1) == (
-        q * col_dev + lax.broadcasted_iota(jnp.int32, (col_dev, columns), 0)
+        lax.broadcasted_iota(jnp.int32, (col_dev, columns), 0) * n_pw + q
     )
     own_x = jnp.sum(jnp.where(own, all_x, 0.0), 1, keepdims=True)
     own_y = jnp.sum(jnp.where(own, all_y, 0.0), 1, keepdims=True)
@@ -310,13 +339,19 @@
     mim_low = jnp.concatenate([ysl, ycl], 1)
 
     out_s[...] = jnp.zeros_like(out_s)
-    base = lax.rem(q, per_tile) * span
 
     take(col_buf, recv_sem.at[0], n_dev - 1)
-    gathered = col_buf[0:n_pw]
-    for b in range(1, n_band):
-        gathered = gathered + col_buf[b * n_pw : (b + 1) * n_pw]
-    col_s[...] = gathered.reshape(columns, 128).T
+    gathered = []
+    for r in range(fold_rows):
+        line = col_buf[:, r, :]
+        total = line[0:n_pw]
+        for b in range(1, n_band):
+            total = total + line[b * n_pw : (b + 1) * n_pw]
+        gathered.append(total)
+    gathered = jnp.concatenate(gathered, 0).T
+    col_s[...] = jnp.concatenate(
+        [gathered[g * span : (g + 1) * span] for g in range(per_tile)], 1
+    )
 
     def own_row():
         ps_recv[me] = ps_send[me]
@@ -338,8 +373,8 @@
         first = step * group
         mixed = []
         for i in range(group):
-            part_re = col_s[pl.ds(base + first + i, 1), :]
-            part_im = col_s[pl.ds(base + span // 2 + first + i, 1), :]
+            part_re = col_s[pl.ds(first + i, 1), :]
+            part_im = col_s[pl.ds(span // 2 + first + i, 1), :]
             mixed.append(
                 jnp.concatenate(
                     [x_cos * part_re - x_sin * part_im, x_cos * part_im + x_sin * part_re], 1
@@ -355,16 +390,21 @@
         for i in range(group):
             back_re = back[i * grid : (i + 1) * grid, :columns]
             back_im = back[i * grid : (i + 1) * grid, columns:]
-            out_s[pl.ds(base + first + i, 1), :] = jnp.sum(
+            out_s[pl.ds(first + i, 1), :] = jnp.sum(
                 x_cos * back_re + x_sin * back_im, 0, keepdims=True
             )
-            out_s[pl.ds(base + span // 2 + first + i, 1), :] = jnp.sum(
+            out_s[pl.ds(span // 2 + first + i, 1), :] = jnp.sum(
                 x_cos * back_im - x_sin * back_re, 0, keepdims=True
             )
         return carry
 
     lax.fori_loop(0, planes // group, some_planes, 0)
-    out_send[...] = out_s[...].T.reshape(n_pw, col_dev, 128)
+    flipped = out_s[...]
+    flipped = jnp.concatenate(
+        [flipped[:, g * piece : (g + 1) * piece] for g in range(per_tile)], 0
+    ).T
+    for r in range(fold_rows):
+        out_send[:, r, :] = flipped[r * n_pw : (r + 1) * n_pw]
     push(lambda band, pw: out_send.at[pw], out_buf.at[me], 3)
     out_buf[me] = out_send[q]
 
@@ -394,7 +434,17 @@
         line = []
         for t in range(tiles):
             begin = b * n_pw + t * per_tile
-            line.append(jnp.sum(out_buf[begin : begin + per_tile], 0))
+            wide = [
+                jnp.concatenate([out_buf[begin + j]] * per_tile, 0) for j in range(per_tile)
+            ]
+            tile = None
+            for d in range(per_tile):
+                part = wide[d]
+                for g in range(1, per_tile):
+                    part = jnp.where(block == g, wide[(g + d) % per_tile], part)
+                part = turned(jnp.where(diagonal, part, 0.0), d)
+                tile = part if tile is None else tile + part
+            line.append(tile)
         lines.append(jnp.concatenate(line, 1))
     lines = jnp.concatenate(lines, 0)
     high, low = halves(lines)
@@ -424,28 +474,54 @@
     span_double = jnp.concatenate(
         [jnp.concatenate([flat_re, flat_im], 1), jnp.concatenate([flat_im, -flat_re], 1)], 0
     )
-    part = exact_dot(doubled(image), span_double, NT) * (1.0 / total_waves)
-    co_send[...] = jnp.zeros_like(co_send)
-    co_send[:, 0 : 2 * vectors] = part
+    count = 2 * slab
+    wide = 2 * vectors
+    folds = slab // co_send.shape[0]
+    row_pad[...] = jnp.zeros_like(row_pad)
+    row_pad[:, 0:wide] = exact_dot(doubled(image)[:slab], span_double, NT) * (
+        1.0 / total_waves
+    )
+    for m in range(slab // folds):
+        line = row_pad[m * folds : m * folds + 1, :]
+        for i in range(1, folds):
+            line = line + pltpu.roll(row_pad[m * folds + i : m * folds + i + 1, :], i * wide, 1)
+        co_send[m : m + 1, :] = line
     push(lambda band, pw: co_send, co_buf.at[me], 4)
     co_buf[me] = co_send[...]
     take(co_buf, recv_sem.at[4], n_dev - 1)
     coef = jnp.sum(co_buf[...], 0)
-    residue = image - exact_dot(coef[:, : 2 * vectors], span_rows, NN)
+    top = []
+    for b in range(slab):
+        line = coef[b // folds : b // folds + 1]
+        if b % folds:
+            line = pltpu.roll(line, 128 - b % folds * wide, 1)
+        top.append(line[:, :wide])
+    top = jnp.concatenate(top, 0)
+    coef = jnp.concatenate(
+        [top, jnp.concatenate([-top[:, vectors:], top[:, :vectors]], 1)], 0
+    )
+    residue = image - exact_dot(coef, span_rows, NN)
 
     residue_double = doubled(residue)
-    part = exact_dot(residue_double, residue_double, NT) * (1.0 / total_waves)
-    gr_send[...] = jnp.zeros_like(gr_send)
-    gr_send[:, 0 : 2 * slab] = part
+    row_pad[...] = jnp.zeros_like(row_pad)
+    row_pad[:, 0:count] = exact_dot(residue_double[:slab], residue_double, NT) * (
+        1.0 / total_waves
+    )
+    line = row_pad[0:1, :]
+    for r in range(1, slab):
+        line = line + pltpu.roll(row_pad[r : r + 1, :], r * count, 1)
+    gr_send[...] = line
     push(lambda band, pw: gr_send, gr_buf.at[me], 5)
     gr_buf[me] = gr_send[...]
 
-    count = 2 * slab
     packed_ref[0:count] = residue
-    packed_ref[count : 2 * count, 0 : coef.shape[1]] = coef
-
+    packed_ref[count : 2 * count, 0:wide] = coef
     take(gr_buf, recv_sem.at[5], n_dev - 1)
-    packed_ref[2 * count : 3 * count, 0:128] = jnp.sum(gr_buf[...], 0)
+    gram = jnp.sum(gr_buf[...], 0)
+    for r in range(slab):
+        packed_ref[2 * count + r : 2 * count + r + 1, 0:128] = (
+            pltpu.roll(gram, 128 - r * count, 1) if r else gram
+        )
 
     take(col_buf, send_sem.at[0], n_dev - 1)
     if rows < n_dev:
@@ -554,40 +630,45 @@
     atoms = atom_sites.shape[1]
     vectors = blocks * slab
     rows = 2 * slab * channels
-    span = 8
+    span = 32
     while span < 2 * planes:
         span *= 2
     group = max(g for g in (1, 2, 3, 4) if planes % g == 0)
-    tiles = n_pw * span // 128
-    wide = -(-2 * vectors // 128) * 128
-    assert slab == n_band and rows <= n_dev and n_pw * span % 128 == 0
+    lanes = n_pw * span
+    fold_rows = col_dev * span // 128
+    messages = max(1, slab * 2 * vectors // 128)
+    assert slab == n_band and rows <= n_dev and lanes % 128 == 0
+    assert span <= 128 and fold_rows * 128 == col_dev * span
+    assert 2 * vectors <= 128 and 2 * slab * slab <= 128 and slab % messages == 0
+    if columns > 512:
+        column_map = column_map.reshape(n_pw, col_dev).T
     tables = host_tables(grid, planes, n_pw, span)
     cfg = (n_band, n_pw, slab, blocks, channels, planes, grid, col_dev, span, group)
     vmem = pl.BlockSpec(memory_space=pltpu.VMEM)
     smem = pl.BlockSpec(memory_space=pltpu.SMEM)
     parts = atoms // 128
     anywhere = pl.BlockSpec(memory_space=pl.ANY)
-    lanes = n_pw * span
     packed = pl.pallas_call(
         functools.partial(kernel, cfg),
-        out_shape=jax.ShapeDtypeStruct((6 * slab, max(waves, wide)), f32),
+        out_shape=jax.ShapeDtypeStruct((6 * slab, max(waves, 128)), f32),
         in_specs=[anywhere] + [vmem] * 4 + [smem] + [vmem] * 5 + [anywhere] * 4,
         out_specs=vmem,
         scratch_shapes=[
-            pltpu.VMEM((slab, tiles, col_dev, 128), f32),
-            pltpu.VMEM((n_dev, col_dev, 128), f32),
-            pltpu.VMEM((128, columns), f32),
+            pltpu.VMEM((slab, n_pw, fold_rows, 128), f32),
+            pltpu.VMEM((n_dev, fold_rows, 128), f32),
+            pltpu.VMEM((span, columns), f32),
             pltpu.VMEM((rows, parts, 128), f32),
             pltpu.VMEM((n_dev, parts, 128), f32),
             pltpu.VMEM((parts, 128), f32),
             pltpu.VMEM((rows, parts, 128), f32),
-            pltpu.VMEM((128, columns), f32),
-            pltpu.VMEM((n_pw, col_dev, 128), f32),
-            pltpu.VMEM((n_dev, col_dev, 128), f32),
-            pltpu.VMEM((2 * slab, wide), f32),
-            pltpu.VMEM((n_dev, 2 * slab, wide), f32),
-            pltpu.VMEM((2 * slab, 128), f32),
-            pltpu.VMEM((n_dev, 2 * slab, 128), f32),
+            pltpu.VMEM((span, columns), f32),
+            pltpu.VMEM((n_pw, fold_rows, 128), f32),
+            pltpu.VMEM((n_dev, fold_rows, 128), f32),
+            pltpu.VMEM((slab, 128), f32),
+            pltpu.VMEM((messages, 128), f32),
+            pltpu.VMEM((n_dev, messages, 128), f32),
+            pltpu.VMEM((1, 128), f32),
+            pltpu.VMEM((n_dev, 1, 128), f32),
             pltpu.VMEM((waves, atoms), bf16),
             pltpu.VMEM((waves, atoms), bf16),
             pltpu.VMEM((planes, grid, grid), f32),

time: 41.1 us -> 39.2 us (0.954)
  Pallas kernels: 40.2 us -> 38.3 us
    pallas_call x1, Pallas kernels: 38.5 us -> 36.7 us  [body(): pl.pallas_call(functools.partial(kernel, cfg), out_shape=jax.ShapeDtypeSt...]
where the time goes in v2:
time: 39.2 us; the launch traced here: 39 us
  Pallas kernels  38.3 us (98%)
  between operations  0.64 us (2%)
    pallas_call x1, Pallas kernels, body(): pl.pallas_call(functools.partial(kernel, cfg), out_shape=jax.ShapeDtypeSt...  36.7 us
    pallas_call x1, Pallas kernels, body(): pl.pallas_call(functools.partial(finish, slab, blocks), out_shape=[jax.Sh...  1.66 us

profile of v2, /device:TPU:0, one launch (start us, length us, event | category | flops | bytes accessed | tf_op | source)
XLA Modules:
  0.0 39.0 jit_solution(233036303739854140)
XLA Ops:
  0.6 36.7 %shard_map.190.packed_ref = f32[12,256]{1,0:T(8,128)} custom-call(f32[12,192,192]{2,1,0:T(8,128)} %pot_ref.1, f32[8,2,1,256]{3,2,1,0:T(1,128)} %basis_re_ref.1, f32[8,2,1,256]{3,2,1,0:T(1,128)} %basis_im_ref.1, f32[2,256]{1,0:T(2,128)} %kin_ref.1, f32[8,2,256]{2,1,0:T(2,128)} %form_ref.1, f32[8]{0:T(128)} %strength_ref.1, s32[2,256]{1,0:T(2,128)} %sphere_ref.1, ...), custom_call_target="tpu_custom_call" | custom-call | tf_op jit(solution)/shard_map/pallas_call | solution.py:651
  37.3 1.7 %shard_map.191 = (f32[2,1,256]{2,1,0:T(1,128)}, f32[2,1,256]{2,1,0:T(1,128)}, f32[2,2,8]{2,1,0:T(2,128)}, f32[2,2,8]{2,1,0:T(2,128)}, f32[2,2]{1,0:T(2,128)}, /*index=5*/f32[2,2]{1,0:T(2,128)}) custom-call(f32[12,256]{1,0:T(8,128)} %shard_map.190.packed_ref), custom_call_target="tpu_custom_call" | custom-call | tf_op jit(solution)/shard_map/pallas_call | solution.py:698

commit v3 on v2

--- a/solution.py
+++ b/solution.py
@@ -140,6 +140,9 @@
     f2l_buf,
     dh_buf,
     dl_buf,
+    fwd_table,
+    back_table,
+    back_left,
     send_sem,
     recv_sem,
     load_sem,
@@ -333,11 +336,21 @@
     x_cos = xch + xcl
     x_sin = xsh + xsl
     ych, ysh, ycl, ysl = [part.astype(bf16) for part in at_columns(all_y)]
+    joined = columns <= 512
     mre_high = jnp.concatenate([ych, -ysh], 1)
     mre_low = jnp.concatenate([ycl, -ysl], 1)
     mim_high = jnp.concatenate([ysh, ych], 1)
     mim_low = jnp.concatenate([ysl, ycl], 1)
 
+    if joined:
+        gap = jnp.zeros((256 - grid, 2 * columns), bf16)
+        high = jnp.concatenate([mre_high, gap, mim_high, gap], 0)
+        low = jnp.concatenate([mre_low, gap, mim_low, gap], 0)
+        fwd_table[...] = jnp.concatenate([high, high, low], 1)
+        back_table[...] = jnp.concatenate(
+            [mre_high, gap, mre_high, gap, mim_high, gap, mim_high, gap, low], 0
+        )
+        back_left[...] = jnp.zeros_like(back_left)
     out_s[...] = jnp.zeros_like(out_s)
 
     take(col_buf, recv_sem.at[0], n_dev - 1)
@@ -352,20 +365,6 @@
     col_s[...] = jnp.concatenate(
         [gathered[g * span : (g + 1) * span] for g in range(per_tile)], 1
     )
-
-    def own_row():
-        ps_recv[me] = ps_send[me]
-        take(ps_recv, recv_sem.at[1], n_dev - 1)
-        total = jnp.sum(ps_recv[...], 0)
-        strength = strength_ref[lax.rem(me, channels)]
-        sc_send[...] = strength * (total * (1.0 / root_waves)) * (1.0 / root_waves)
-        sc_buf[me] = sc_send[...]
-        push(lambda band, pw: sc_send, sc_buf.at[me], 2)
-
-    if rows < n_dev:
-        pl.when(me < rows)(own_row)
-    else:
-        own_row()
 
     loads[2].wait()
 
@@ -381,12 +380,23 @@
                 )
             )
         mixed = jnp.concatenate(mixed, 0)
-        field_re = dot_split(mixed, mre_high, mre_low, NT)
-        field_im = dot_split(mixed, mim_high, mim_low, NT)
         weight = pot_buf[pl.ds(first, group)].reshape(group * grid, grid)
-        back = dot_split(field_re * weight, mre_high, mre_low, NN) + dot_split(
-            field_im * weight, mim_high, mim_low, NN
-        )
+        if joined:
+            high, low = halves(mixed)
+            field = dot(jnp.concatenate([high, low, high], 1), fwd_table[...], NT)
+            re_high, re_low = halves(field[:, :grid] * weight)
+            im_high, im_low = halves(field[:, 256 : 256 + grid] * weight)
+            for i, part in enumerate((re_low, re_high, im_high, im_low)):
+                back_left[:, i * 256 : i * 256 + grid] = part
+            back = dot(back_left[...], back_table[0:1024], NN) + dot(
+                back_left[:, 256:768], back_table[1024:1536], NN
+            )
+        else:
+            field_re = dot_split(mixed, mre_high, mre_low, NT)
+            field_im = dot_split(mixed, mim_high, mim_low, NT)
+            back = dot_split(field_re * weight, mre_high, mre_low, NN) + dot_split(
+                field_im * weight, mim_high, mim_low, NN
+            )
         for i in range(group):
             back_re = back[i * grid : (i + 1) * grid, :columns]
             back_im = back[i * grid : (i + 1) * grid, columns:]
@@ -398,7 +408,24 @@
             )
         return carry
 
-    lax.fori_loop(0, planes // group, some_planes, 0)
+    some_planes(0, 0)
+
+    def own_row():
+        ps_recv[me] = ps_send[me]
+        take(ps_recv, recv_sem.at[1], n_dev - 1)
+        total = jnp.sum(ps_recv[...], 0)
+        strength = strength_ref[lax.rem(me, channels)]
+        sc_send[...] = strength * (total * (1.0 / root_waves)) * (1.0 / root_waves)
+        sc_buf[me] = sc_send[...]
+        push(lambda band, pw: sc_send, sc_buf.at[me], 2)
+
+    if rows < n_dev:
+        pl.when(me < rows)(own_row)
+    else:
+        own_row()
+
+    if planes > group:
+        lax.fori_loop(1, planes // group, some_planes, 0)
     flipped = out_s[...]
     flipped = jnp.concatenate(
         [flipped[:, g * piece : (g + 1) * piece] for g in range(per_tile)], 0
@@ -637,7 +664,7 @@
     lanes = n_pw * span
     fold_rows = col_dev * span // 128
     messages = max(1, slab * 2 * vectors // 128)
-    assert slab == n_band and rows <= n_dev and lanes % 128 == 0
+    assert grid <= 256 and slab == n_band and rows <= n_dev and lanes % 128 == 0
     assert span <= 128 and fold_rows * 128 == col_dev * span
     assert 2 * vectors <= 128 and 2 * slab * slab <= 128 and slab % messages == 0
     if columns > 512:
@@ -676,6 +703,14 @@
             pltpu.VMEM((2, lanes, grid), bf16),
             pltpu.VMEM((2, grid, grid), bf16),
             pltpu.VMEM((2, grid, grid), bf16),
+            *[
+                pltpu.VMEM(shape if columns <= 512 else (16, 128), bf16)
+                for shape in (
+                    (512, 6 * columns),
+                    (1536, 2 * columns),
+                    (group * grid, 1024),
+                )
+            ],
             pltpu.SemaphoreType.DMA((6,)),
             pltpu.SemaphoreType.DMA((6,)),
             pltpu.SemaphoreType.DMA((5,)),

time: 39.2 us -> 39 us (level)
  no operation moved by 1% of the time
where the time goes in v3:
time: 39 us; the launch traced here: 38.7 us
  Pallas kernels  38.1 us (98%)
  between operations  0.64 us (2%)
    pallas_call x1, Pallas kernels, body(): pl.pallas_call(functools.partial(kernel, cfg), out_shape=jax.ShapeDtypeSt...  36.4 us
    pallas_call x1, Pallas kernels, body(): pl.pallas_call(functools.partial(finish, slab, blocks), out_shape=[jax.Sh...  1.66 us

profile of v3, /device:TPU:0, one launch (start us, length us, event | category | flops | bytes accessed | tf_op | source)
XLA Modules:
  0.0 38.7 jit_solution(6583180114747722129)
XLA Ops:
  0.6 36.4 %shard_map.190.packed_ref = f32[12,256]{1,0:T(8,128)} custom-call(f32[12,192,192]{2,1,0:T(8,128)} %pot_ref.1, f32[8,2,1,256]{3,2,1,0:T(1,128)} %basis_re_ref.1, f32[8,2,1,256]{3,2,1,0:T(1,128)} %basis_im_ref.1, f32[2,256]{1,0:T(2,128)} %kin_ref.1, f32[8,2,256]{2,1,0:T(2,128)} %form_ref.1, f32[8]{0:T(128)} %strength_ref.1, s32[2,256]{1,0:T(2,128)} %sphere_ref.1, ...), custom_call_target="tpu_custom_call" | custom-call | tf_op jit(solution)/shard_map/pallas_call | solution.py:678
  37.1 1.7 %shard_map.191 = (f32[2,1,256]{2,1,0:T(1,128)}, f32[2,1,256]{2,1,0:T(1,128)}, f32[2,2,8]{2,1,0:T(2,128)}, f32[2,2,8]{2,1,0:T(2,128)}, f32[2,2]{1,0:T(2,128)}, /*index=5*/f32[2,2]{1,0:T(2,128)}) custom-call(f32[12,256]{1,0:T(8,128)} %shard_map.190.packed_ref), custom_call_target="tpu_custom_call" | custom-call | tf_op jit(solution)/shard_map/pallas_call | solution.py:733

commit v4 on v3

--- a/solution.py
+++ b/solution.py
@@ -169,14 +169,18 @@
         return jnp.where(value >= size, value - size, value)
 
     def others(act):
-        for turn in range(n_band):
+        for turn in reversed(range(n_band)):
             band = wrap(s + turn, n_band)
 
             def one(k, carry):
                 act(band, wrap(q + k, n_pw))
                 return carry
 
-            lax.fori_loop(1, n_pw, one, 0, unroll=n_dev <= 64)
+            if n_dev <= 64:
+                for k in sorted(range(1, n_pw), key=lambda k: -min(k, n_pw - k)):
+                    one(k, 0)
+            else:
+                lax.fori_loop(1, n_pw, one, 0)
             if turn:
                 act(band, q)
 
@@ -542,7 +546,10 @@
     gr_buf[me] = gr_send[...]
 
     packed_ref[0:count] = residue
-    packed_ref[count : 2 * count, 0:wide] = coef
+    lane_out = lax.broadcasted_iota(jnp.int32, (vectors, vectors), 0)
+    lane_in = lax.broadcasted_iota(jnp.int32, (vectors, vectors), 1)
+    order = (lane_in == lax.rem(lane_out, blocks) * slab + lane_out // blocks).astype(f32)
+    packed_ref[count : 2 * count, 0:vectors] = exact_dot(coef[:, :vectors], order, NT)
     take(gr_buf, recv_sem.at[5], n_dev - 1)
     gram = jnp.sum(gr_buf[...], 0)
     for r in range(slab):
@@ -578,15 +585,8 @@
     vectors = blocks * slab
     residue = packed_ref[0:count]
     gram = packed_ref[2 * count : 3 * count, 0:128]
-    pick = (
-        lax.broadcasted_iota(jnp.int32, (slab * blocks, vectors), 0),
-        lax.broadcasted_iota(jnp.int32, (slab * blocks, vectors), 1),
-    )
-    order = (pick[1] == lax.rem(pick[0], blocks) * slab + pick[0] // blocks).astype(f32)
     for part, ref in ((0, coef_re_ref), (slab, coef_im_ref)):
-        line = exact_dot(
-            packed_ref[count + part : count + part + slab, 0:vectors], order, NT
-        )
+        line = packed_ref[count + part : count + part + slab, 0:vectors]
         for k in range(slab):
             ref[k] = line[:, k * blocks : (k + 1) * blocks]
 

time: 39 us -> 38.8 us (level)
  no operation moved by 1% of the time
where the time goes in v4:
time: 38.8 us; the launch traced here: 38.5 us
  Pallas kernels  37.9 us (98%)
  between operations  0.64 us (2%)
    pallas_call x1, Pallas kernels, body(): pl.pallas_call(functools.partial(kernel, cfg), out_shape=jax.ShapeDtypeSt...  36.2 us
    pallas_call x1, Pallas kernels, body(): pl.pallas_call(functools.partial(finish, slab, blocks), out_shape=[jax.Sh...  1.66 us

profile of v4, /device:TPU:0, one launch (start us, length us, event | category | flops | bytes accessed | tf_op | source)
XLA Modules:
  0.0 38.5 jit_solution(6695743147166182427)
XLA Ops:
  0.6 36.2 %shard_map.190.packed_ref = f32[12,256]{1,0:T(8,128)} custom-call(f32[12,192,192]{2,1,0:T(8,128)} %pot_ref.1, f32[8,2,1,256]{3,2,1,0:T(1,128)} %basis_re_ref.1, f32[8,2,1,256]{3,2,1,0:T(1,128)} %basis_im_ref.1, f32[2,256]{1,0:T(2,128)} %kin_ref.1, f32[8,2,256]{2,1,0:T(2,128)} %form_ref.1, f32[8]{0:T(128)} %strength_ref.1, s32[2,256]{1,0:T(2,128)} %sphere_ref.1, ...), custom_call_target="tpu_custom_call" | custom-call | tf_op jit(solution)/shard_map/pallas_call | solution.py:678
  36.9 1.7 %shard_map.191 = (f32[2,1,256]{2,1,0:T(1,128)}, f32[2,1,256]{2,1,0:T(1,128)}, f32[2,2,8]{2,1,0:T(2,128)}, f32[2,2,8]{2,1,0:T(2,128)}, f32[2,2]{1,0:T(2,128)}, /*index=5*/f32[2,2]{1,0:T(2,128)}) custom-call(f32[12,256]{1,0:T(8,128)} %shard_map.190.packed_ref), custom_call_target="tpu_custom_call" | custom-call | tf_op jit(solution)/shard_map/pallas_call | solution.py:733
